TPU v7x, 32 devices: a whole 2x2x4 slice. The times are simulated.
32 devices in a mesh: col: 4 (over z), row: 8 (over y, x, core).
Axes of the slice: x: 2, y: 2, z: 4, core: 2. Of those that a mesh axis runs over, the one named last changes fastest.
Arguments:
- factor: float32 [8192, 2048], P('row', 'col'), may hold values from -100 to 100
- support: int32 [16, 64], P(None, 'row'), may hold values from 0 to 1, as said below
- plan: int32 [2, 16], replicated, may hold values from 0 to 15, as said below
Outputs:
- rotated_factor: float32 [8192, 2048], P('row', 'col')
Inputs may be any that keep to these rules, and one draw needn't show every extreme that they name: Every column block has at least one row block in its support. `plan`: each row is a permutation; cut each round's row into groups of 4 consecutive positions (group g on index g of col); the 4 blocks of any group sit in 4 different groups of the previous round's row, where the order before round 0 is 0, 1, ..., 15.
All inputs are finite; a program needn't handle non-finite values.
Results may differ from a plain program's by a relative error of at most 0.0003.
Values sent between devices are 32-bit elements; how exact they have to be, the bound alone decides.
A program may use at most 128 MiB of HBM per device.

v0:
```python
import functools

import jax
import jax.numpy as jnp
from jax import lax
from jax.experimental import pallas as pl
from jax.experimental.pallas import tpu as pltpu
from jax.sharding import PartitionSpec as P

W = 128
RB = 128
ROUNDS = 2
CHUNKS = 4
SCALED_STEPS = 7
TRUE_STEPS = 2
DAMPING = 0.01
F32 = jnp.float32
BF16 = jnp.bfloat16
MESH = pl.DeviceIdType.MESH


def split(x):
    high = x.astype(BF16)
    return high, (x - high.astype(F32)).astype(BF16)


def dot(a, b):
    return jnp.dot(a, b, preferred_element_type=F32)


def dot3(a, b):
    a_high, a_low = split(a)
    b_high, b_low = split(b)
    return dot(a_high, b_high) + (dot(a_high, b_low) + dot(a_low, b_high))


def dot_t(a, b):
    return lax.dot_general(a, b, (((0,), (0,)), ((), ())), preferred_element_type=F32)


def rotation(gram, eye, stack):
    size = gram.shape[0]
    on_diagonal = gram * eye
    diag_rows = jnp.sum(on_diagonal, axis=1, keepdims=True)
    diag_cols = jnp.sum(on_diagonal, axis=0, keepdims=True)
    spread = diag_rows - diag_cols
    joined = diag_rows + diag_cols
    half = 0.5 * gram * spread / (spread * spread + gram * gram + DAMPING * joined * joined)
    squared = dot3(half, half)
    total = jnp.sum(jnp.sum(squared * squared, axis=1, keepdims=True), axis=0, keepdims=True)
    upper = 1.0 + 1.001 * jnp.sqrt(0.5 * total)
    stack[:size] = eye - squared
    stack[size:] = eye - half

    def scaled(_, bounds):
        low, high = bounds
        scale = 2.0 / (low + high)
        delta = (high - low) / (high + low)
        factor = (2.0 * scale) * eye - (scale * scale) * stack[:size]
        stack[...] = dot3(stack[...], factor)
        return 1.0 - delta * delta, jnp.ones_like(high)

    lax.fori_loop(0, SCALED_STEPS, scaled, (jnp.ones_like(upper), upper))

    def true(_, carry):
        inverse = stack[size:]
        residual = (eye - inverse) - dot3(half, inverse)
        stack[size:] = inverse + dot3(inverse, residual)
        return carry

    lax.fori_loop(0, TRUE_STEPS, true, 0)
    return 2.0 * stack[size:] - eye


def pack(gram):
    first, last = gram[:W, :W], gram[W:, W:]
    row_ids = lax.broadcasted_iota(jnp.int32, (W, W), 0)
    col_ids = lax.broadcasted_iota(jnp.int32, (W, W), 1)
    tile = jnp.where(row_ids >= col_ids, first, last)
    diagonal = jnp.sum(jnp.where(row_ids == col_ids, last, 0.0), axis=0, keepdims=True)
    return gram[:W, W:], tile, jnp.broadcast_to(diagonal, (8, W))


def unpack(packed):
    cross, tile, diagonal = packed[:W], packed[W:2 * W], packed[2 * W:2 * W + 1]
    row_ids = lax.broadcasted_iota(jnp.int32, (W, W), 0)
    col_ids = lax.broadcasted_iota(jnp.int32, (W, W), 1)
    lower = jnp.where(row_ids > col_ids, tile, 0.0)
    upper = jnp.where(row_ids < col_ids, tile, 0.0)
    first = lower + lower.T + jnp.where(row_ids == col_ids, tile, 0.0)
    last = upper + upper.T + jnp.where(row_ids == col_ids, diagonal, 0.0)
    top = jnp.concatenate([first, cross], axis=1)
    return jnp.concatenate([top, jnp.concatenate([cross.T, last], axis=1)], axis=0)


def kernel(
    groups, members, factor_ref, support_ref, plan_ref, out_ref,
    held, cur, send, recv, early_out, early_in, turn_out, turns,
    acc, gram, gram_in, rot, rot_pair, stack,
    load_sem, move_send, move_recv, early_send, early_recv, turn_send, turn_recv, spread_send, spread_recv,
    swap_send, swap_recv, sum_send, sum_recv, rot_send, rot_recv,
):
    slots, rows, _ = cur.shape
    size = 2 * W
    chunk = rows // CHUNKS
    chips = members // 2
    stages = chips.bit_length() - 1
    g = lax.axis_index("col")
    m = lax.axis_index("row")
    core = lax.rem(m, 2)
    chip = m // 2
    partner = m + 1 - 2 * core

    def flipped(bit):
        step = 1 << bit
        on = lax.rem(chip // step, 2)
        return (chip + step - 2 * step * on) * 2 + core

    loads = []
    for q in range(CHUNKS):
        span = pl.ds(q * chunk, chunk)
        loads.append(pltpu.make_async_copy(factor_ref.at[span], held.at[span], load_sem.at[q]))
        loads[q].start()

    peers = [{"col": lax.rem(g + o, groups), "row": m} for o in range(1, groups)]
    peers += [{"col": g, "row": partner}]
    peers += [{"col": g, "row": flipped(b)} for b in range(stages)]
    barrier = pltpu.get_barrier_semaphore()
    for peer in peers:
        pl.semaphore_signal(barrier, inc=1, device_id=peer, device_id_type=MESH)

    row_ids = lax.broadcasted_iota(jnp.int32, (size, size), 0)
    col_ids = lax.broadcasted_iota(jnp.int32, (size, size), 1)
    eye = (row_ids == col_ids).astype(F32)

    def mask(q):
        loads[q].wait()
        for s in range(slots):
            for b in range(q * chunk // RB, (q + 1) * chunk // RB):
                span = pl.ds(b * RB, RB)
                weight = support_ref[b, g * slots + s].astype(F32)
                cur[s, span] = held[span, s * W:(s + 1) * W] * weight

    def before(r, position):
        return position if r == 0 else plan_ref[r - 1, position]

    blocks = groups * slots
    pick, take = [], []
    for r in range(ROUNDS):
        dest = []
        for s in range(slots):
            block = before(r, g * slots + s)
            dest.append(sum(
                jnp.where(plan_ref[r, j] == block, j // slots, 0) for j in range(blocks)))
        pick.append([
            jnp.minimum(slots - 1, sum(
                jnp.where(dest[s] == lax.rem(g + o, groups), s, 0) for s in range(slots)))
            for o in range(groups)])
        take.append([])
        for s in range(slots):
            block = plan_ref[r, g * slots + s]
            take[r].append(jnp.minimum(groups - 1, sum(
                jnp.where(before(r, j) == block, j // slots, 0) for j in range(blocks))))

    pl.semaphore_wait(barrier, len(peers))

    copies, stores = [], []

    def start(copy):
        copy.start()
        copies.append(copy)
        return copy

    def dispatch(r, q):
        span = pl.ds(q * chunk, chunk)
        out = []
        for o in range(1, groups):
            send[r, o - 1, span] = cur[pick[r][o], span]
            out.append(start(pltpu.make_async_remote_copy(
                src_ref=send.at[r, o - 1, span],
                dst_ref=recv[r][q].at[g],
                send_sem=move_send.at[r, q, o - 1],
                recv_sem=move_recv.at[r, q, o - 1],
                device_id=peers[o - 1],
                device_id_type=MESH,
            )))
        recv[r][q][g] = cur[pick[r][0], span]
        return out

    def load_pair(r, k, q):
        held = recv[r][q]
        return jnp.concatenate([held[take[r][2 * k]], held[take[r][2 * k + 1]]], axis=1)

    def stage_early():
        for o in range(1, groups):
            second = pick[1][o] // 2 == 1
            left = jnp.where(second, take[0][2], take[0][0])
            right = jnp.where(second, take[0][3], take[0][1])
            early_out[o - 1, :, :W] = recv[0][0][left]
            early_out[o - 1, :, W:] = recv[0][0][right]

    def send_early():
        return [start(pltpu.make_async_remote_copy(
            src_ref=early_out.at[o - 1],
            dst_ref=early_in.at[o - 1],
            send_sem=early_send.at[o - 1],
            recv_sem=early_recv.at[o - 1],
            device_id=peers[o - 1],
            device_id_type=MESH,
        )) for o in range(1, groups)]

    share = size // members
    mine = pl.ds(pl.multiple_of(m * share, share), share)

    def send_turns():
        out = []
        for o in range(1, groups):
            wide = rot_pair[pick[1][o] // 2, mine]
            turn_out[o - 1] = jnp.where(lax.rem(pick[1][o], 2) == 0, wide[:, :W], wide[:, W:])
            out.append(start(pltpu.make_async_remote_copy(
                src_ref=turn_out.at[o - 1],
                dst_ref=turns.at[o - 1, mine],
                send_sem=turn_send.at[o - 1],
                recv_sem=turn_recv.at[o - 1],
                device_id=peers[o - 1],
                device_id_type=MESH,
            )))
        return out

    def finish_early(turned, early):
        for copy in turned:
            copy.wait_recv()
        for b in range(stages + 1):
            span = pl.ds(pl.multiple_of((m // (1 << b)) * (1 << b) * share, share), share << b)
            start(pltpu.make_async_remote_copy(
                src_ref=turns.at[:, span],
                dst_ref=turns.at[:, span],
                send_sem=spread_send.at[b],
                recv_sem=spread_recv.at[b],
                device_id=peers[groups - 1 + b],
                device_id_type=MESH,
            )).wait_recv()
        for o in range(1, groups):
            early[o - 1].wait_recv()
            source = lax.rem(g + groups - o, groups)
            recv[1][0][source] = dot3(early_in[o - 1], turns[o - 1])

    moves = []
    for q in range(CHUNKS):
        mask(q)
        moves.append(dispatch(0, q))
    for r in range(ROUNDS):
        for q in range(CHUNKS):
            for copy in moves[q]:
                copy.wait_recv()
            if r == 0 and q == CHUNKS - 1:
                early = send_early()
            for k in range(2):
                high, low = split(load_pair(r, k, q))
                mixed = dot_t(high, low)
                part = dot_t(high, high) + (mixed + mixed.T)
                acc[k] = part if q == 0 else acc[k] + part
            if r == 0 and q == 0:
                stage_early()
        for k in range(2):
            cross, tile, diagonal = pack(acc[k])
            gram_in[r, k, :W] = cross
            gram_in[r, k, W:size] = tile
            gram_in[r, k, size:] = diagonal
        swap = start(pltpu.make_async_remote_copy(
            src_ref=gram_in.at[r, 1 - core],
            dst_ref=gram_in.at[r, 2],
            send_sem=swap_send.at[r],
            recv_sem=swap_recv.at[r],
            device_id=peers[groups - 1],
            device_id_type=MESH,
        ))
        swap.wait_recv()
        total = gram_in[r, core] + gram_in[r, 2]
        for stage in range(stages):
            gram[r, 2 * stage] = total
            pair = []
            for h in range(2):
                bit = (stage + h * (stages // 2)) % stages
                part = pl.ds(0, W) if h == 0 else pl.ds(W, W + 8)
                pair.append(start(pltpu.make_async_remote_copy(
                    src_ref=gram.at[r, 2 * stage, part],
                    dst_ref=gram.at[r, 2 * stage + 1, part],
                    send_sem=sum_send.at[r, stage, h],
                    recv_sem=sum_recv.at[r, stage, h],
                    device_id=peers[groups + bit],
                    device_id_type=MESH,
                )))
            for copy in pair:
                copy.wait_recv()
            total = total + gram[r, 2 * stage + 1]
        rot[r, 0] = rotation(unpack(total), eye, stack)
        back = start(pltpu.make_async_remote_copy(
            src_ref=rot.at[r, 0],
            dst_ref=rot.at[r, 1],
            send_sem=rot_send.at[r],
            recv_sem=rot_recv.at[r],
            device_id=peers[groups - 1],
            device_id_type=MESH,
        ))
        back.wait_recv()
        rot_pair[core] = rot[r, 0]
        rot_pair[1 - core] = rot[r, 1]
        moves = []
        if r < ROUNDS - 1:
            turned_copies = send_turns()
        for q in (range(CHUNKS) if r == ROUNDS - 1 else [*range(1, CHUNKS), 0]):
            span = pl.ds(q * chunk, chunk)
            for k in range(2):
                turned = dot3(load_pair(r, k, q), rot_pair[k])
                if r == ROUNDS - 1:
                    held[span, k * size:(k + 1) * size] = turned
                else:
                    cur[2 * k, span] = turned[:, :W]
                    cur[2 * k + 1, span] = turned[:, W:]
            if r == ROUNDS - 1:
                stores.append(pltpu.make_async_copy(held.at[span], out_ref.at[span], load_sem.at[q]))
                stores[q].start()
            elif q > 0:
                moves.append(dispatch(r + 1, q))
            else:
                recv[1][0][g] = cur[pick[1][0], span]
                finish_early(turned_copies, early)
                moves.insert(0, [])
    for copy in copies:
        copy.wait_send()
    for copy in stores:
        copy.wait()


def on_device(groups, members, factor, support, plan):
    rows = factor.shape[0]
    slots = factor.shape[1] // W
    chips = members // 2
    stages = chips.bit_length() - 1
    assert slots == 4 and chips == 1 << stages and stages >= 1 and ROUNDS == 2
    size = 2 * W
    dma = pltpu.SemaphoreType.DMA
    smem = pl.BlockSpec(memory_space=pltpu.SMEM)
    return pl.pallas_call(
        functools.partial(kernel, groups, members),
        out_shape=jax.ShapeDtypeStruct(factor.shape, F32),
        in_specs=[pl.BlockSpec(memory_space=pl.ANY), smem, smem],
        out_specs=pl.BlockSpec(memory_space=pl.ANY),
        scratch_shapes=[
            pltpu.VMEM(factor.shape, F32),
            pltpu.VMEM((slots, rows, W), F32),
            pltpu.VMEM((ROUNDS, groups - 1, rows, W), F32),
            [[pltpu.VMEM((groups, rows // CHUNKS, W), F32)] * CHUNKS] * ROUNDS,
            pltpu.VMEM((groups - 1, rows // CHUNKS, size), F32),
            pltpu.VMEM((groups - 1, rows // CHUNKS, size), F32),
            pltpu.VMEM((groups - 1, size // members, W), F32),
            pltpu.VMEM((groups - 1, size, W), F32),
            pltpu.VMEM((2, size, size), F32),
            pltpu.VMEM((ROUNDS, 2 * stages, size + 8, W), F32),
            pltpu.VMEM((ROUNDS, 3, size + 8, W), F32),
            pltpu.VMEM((ROUNDS, 2, size, size), F32),
            pltpu.VMEM((2, size, size), F32),
            pltpu.VMEM((2 * size, size), F32),
            dma((CHUNKS,)),
            dma((ROUNDS, CHUNKS, groups - 1)),
            dma((ROUNDS, CHUNKS, groups - 1)),
            dma((groups - 1,)),
            dma((groups - 1,)),
            dma((groups - 1,)),
            dma((groups - 1,)),
            dma((stages + 1,)),
            dma((stages + 1,)),
            dma((ROUNDS,)),
            dma((ROUNDS,)),
            dma((ROUNDS, stages, 2)),
            dma((ROUNDS, stages, 2)),
            dma((ROUNDS,)),
            dma((ROUNDS,)),
        ],
        compiler_params=pltpu.CompilerParams(
            collective_id=0, has_side_effects=True, vmem_limit_bytes=123 * 512 * 1024
        ),
    )(factor, support.T, plan)


def solution(mesh):
    return jax.shard_map(
        functools.partial(on_device, mesh.shape["col"], mesh.shape["row"]),
        mesh=mesh,
        in_specs=(P("row", "col"), P(None, "row"), P()),
        out_specs=P("row", "col"),
        check_vma=False,
    )
```

profile of v0, /device:TPU:1, one launch (start us, length us, event | category | flops | bytes accessed | tf_op | source)
XLA Modules:
  0.0 128.5 jit_solution(16658480841042050754)
XLA Ops:
  0.0 125.4 %shard_map.37 = f32[1024,512]{1,0:T(8,128)} custom-call(f32[1024,512]{1,0:T(8,128)} %factor_ref.1, s32[8,16]{1,0:T(8,128)} %bitcast.1, s32[2,16]{1,0:T(2,128)} %plan_ref.1), custom_call_target="tpu_custom_call" | custom-call | tf_op jit(solution)/shard_map/pallas_call | solution.py:345
  125.4 3.1 %copy.5 = f32[1024,512]{1,0:T(8,128)} copy(f32[1024,512]{1,0:T(8,128)} %shard_map.37) | data formatting | bytes 4194304
where the time goes:
time: 129 us; the launch traced here: 128 us
  Pallas kernels  125 us (97%)
  local copies, waits for them, and re-layouts  3.08 us (2%)
    pallas_call x1, Pallas kernels, on_device(): pl.pallas_call(functools.partial(kernel, groups, members), out_shape=jax....  125 us
    unnamed x1, local copies, waits for them, and re-layouts  3.08 us

commit v1 on v0

v1 whole, which is shorter than its diff:
```python
import functools

import jax
import jax.numpy as jnp
from jax import lax
from jax.experimental import pallas as pl
from jax.experimental.pallas import tpu as pltpu
from jax.sharding import PartitionSpec as P

W = 128
RB = 128
ROUNDS = 2
CHUNKS = 4
SCALED_STEPS = 7
TRUE_STEPS = 2
DAMPING = 0.01
F32 = jnp.float32
BF16 = jnp.bfloat16
MESH = pl.DeviceIdType.MESH


def split(x):
    high = x.astype(BF16)
    return high, (x - high.astype(F32)).astype(BF16)


def dot(a, b):
    return jnp.dot(a, b, preferred_element_type=F32)


def dot3(a, b):
    a_high, a_low = split(a)
    b_high, b_low = split(b)
    return dot(a_high, b_high) + (dot(a_high, b_low) + dot(a_low, b_high))


def dot_t(a, b):
    return lax.dot_general(a, b, (((0,), (0,)), ((), ())), preferred_element_type=F32)


def rotation(gram, eye, stack):
    size = gram.shape[0]
    on_diagonal = gram * eye
    diag_rows = jnp.sum(on_diagonal, axis=1, keepdims=True)
    diag_cols = jnp.sum(on_diagonal, axis=0, keepdims=True)
    spread = diag_rows - diag_cols
    joined = diag_rows + diag_cols
    half = 0.5 * gram * spread / (spread * spread + gram * gram + DAMPING * joined * joined)
    squared = dot3(half, half)
    total = jnp.sum(jnp.sum(squared * squared, axis=1, keepdims=True), axis=0, keepdims=True)
    upper = 1.0 + 1.001 * jnp.sqrt(0.5 * total)
    stack[:size] = eye - squared
    stack[size:] = eye - half

    def scaled(_, bounds):
        low, high = bounds
        scale = 2.0 / (low + high)
        delta = (high - low) / (high + low)
        factor = (2.0 * scale) * eye - (scale * scale) * stack[:size]
        stack[...] = dot3(stack[...], factor)
        return 1.0 - delta * delta, jnp.ones_like(high)

    lax.fori_loop(0, SCALED_STEPS, scaled, (jnp.ones_like(upper), upper))

    def true(_, carry):
        inverse = stack[size:]
        residual = (eye - inverse) - dot3(half, inverse)
        stack[size:] = inverse + dot3(inverse, residual)
        return carry

    lax.fori_loop(0, TRUE_STEPS, true, 0)
    return 2.0 * stack[size:] - eye


def pack(gram):
    first, last = gram[:W, :W], gram[W:, W:]
    row_ids = lax.broadcasted_iota(jnp.int32, (W, W), 0)
    col_ids = lax.broadcasted_iota(jnp.int32, (W, W), 1)
    tile = jnp.where(row_ids >= col_ids, first, last)
    diagonal = jnp.sum(jnp.where(row_ids == col_ids, last, 0.0), axis=0, keepdims=True)
    return gram[:W, W:], tile, jnp.broadcast_to(diagonal, (8, W))


def unpack(packed):
    cross, tile, diagonal = packed[:W], packed[W:2 * W], packed[2 * W:2 * W + 1]
    row_ids = lax.broadcasted_iota(jnp.int32, (W, W), 0)
    col_ids = lax.broadcasted_iota(jnp.int32, (W, W), 1)
    lower = jnp.where(row_ids > col_ids, tile, 0.0)
    upper = jnp.where(row_ids < col_ids, tile, 0.0)
    first = lower + lower.T + jnp.where(row_ids == col_ids, tile, 0.0)
    last = upper + upper.T + jnp.where(row_ids == col_ids, diagonal, 0.0)
    top = jnp.concatenate([first, cross], axis=1)
    return jnp.concatenate([top, jnp.concatenate([cross.T, last], axis=1)], axis=0)


def kernel(
    groups, members, factor_ref, support_ref, plan_ref, out_ref,
    held, cur, send, recv, acc, gram, gram_in, rot, stack,
    load_sem, store_sem, move_send, move_recv, swap_send, swap_recv, sum_send, sum_recv, rot_send, rot_recv,
):
    slots, rows, _ = cur.shape
    size = 2 * W
    chunk = rows // CHUNKS
    chips = members // 2
    stages = chips.bit_length() - 1
    g = lax.axis_index("col")
    m = lax.axis_index("row")
    core = lax.rem(m, 2)
    chip = m // 2
    partner = m + 1 - 2 * core
    half = g // 2
    goals = [2 - half, g + 1 - 2 * lax.rem(g, 2), 3 - 3 * half]

    def flipped(bit):
        step = 1 << bit
        on = lax.rem(chip // step, 2)
        return (chip + step - 2 * step * on) * 2 + core

    loads = []
    for q in range(CHUNKS):
        span = pl.ds(q * chunk, chunk)
        loads.append(pltpu.make_async_copy(factor_ref.at[span], held.at[span], load_sem.at[q]))
        loads[q].start()

    goal_peers = [{"col": goal, "row": m} for goal in goals]
    row_peers = [{"col": g, "row": partner}]
    row_peers += [{"col": g, "row": flipped(b)} for b in range(stages)]
    barrier = pltpu.get_barrier_semaphore()
    for peer in goal_peers + row_peers:
        pl.semaphore_signal(barrier, inc=1, device_id=peer, device_id_type=MESH)

    row_ids = lax.broadcasted_iota(jnp.int32, (size, size), 0)
    col_ids = lax.broadcasted_iota(jnp.int32, (size, size), 1)
    eye = (row_ids == col_ids).astype(F32)

    def mask(q):
        loads[q].wait()
        for s in range(slots):
            for b in range(q * chunk // RB, (q + 1) * chunk // RB):
                span = pl.ds(b * RB, RB)
                weight = support_ref[b, g * slots + s].astype(F32)
                cur[s, span] = held[span, s * W:(s + 1) * W] * weight

    def before(r, position):
        return position if r == 0 else plan_ref[r - 1, position]

    blocks = groups * slots
    pick, keep, take = [], [], []
    for r in range(ROUNDS):
        dest = []
        for s in range(slots):
            block = before(r, g * slots + s)
            dest.append(sum(
                jnp.where(plan_ref[r, j] == block, j // slots, 0) for j in range(blocks)))

        def slot_for(goal):
            return jnp.minimum(slots - 1, sum(
                jnp.where(dest[s] == goal, s, 0) for s in range(slots)))

        pick.append([slot_for(goal) for goal in goals])
        keep.append(slot_for(g))
        take.append([])
        for s in range(slots):
            block = plan_ref[r, g * slots + s]
            take[r].append(jnp.minimum(groups - 1, sum(
                jnp.where(before(r, j) == block, j // slots, 0) for j in range(blocks))))

    copies, stores = [], []

    def start(copy):
        copy.start()
        copies.append(copy)
        return copy

    def move(r, q, j, source):
        span = pl.ds(q * chunk, chunk)
        return pltpu.make_async_remote_copy(
            src_ref=send.at[r, j, span],
            dst_ref=recv[r][q].at[source],
            send_sem=move_send.at[r, q, j],
            recv_sem=move_recv.at[r, q, source],
            device_id=goal_peers[j],
            device_id_type=MESH,
        )

    def prepare(r, q):
        span = pl.ds(q * chunk, chunk)
        for j in range(groups - 1):
            send[r, j, span] = cur[pick[r][j], span]
        recv[r][q][g] = cur[keep[r], span]

    def arrive(r, q):
        for o in range(1, groups):
            move(r, q, 0, lax.rem(g + o, groups)).wait_recv()

    def load_pair(r, k, q):
        first = jnp.where(k == 0, take[r][0], take[r][2])
        last = jnp.where(k == 0, take[r][1], take[r][3])
        return jnp.concatenate([recv[r][q][first], recv[r][q][last]], axis=1)

    mask(0)
    prepare(0, 0)
    pl.semaphore_wait(barrier, groups - 1 + len(row_peers))
    for q in range(CHUNKS):
        if q:
            mask(q)
            prepare(0, q)
        for j in range(groups - 2):
            start(move(0, q, j, g))
    for q in range(CHUNKS):
        start(move(0, q, groups - 2, g))
    for r in range(ROUNDS):
        for q in range(CHUNKS):
            arrive(r, q)
            for k in range(2):
                high, low = split(load_pair(r, k, q))
                mixed = dot_t(high, low)
                part = dot_t(high, high) + (mixed + mixed.T)
                acc[k] = part if q == 0 else acc[k] + part
        for k in range(2):
            cross, tile, diagonal = pack(acc[k])
            gram_in[r, k, :W] = cross
            gram_in[r, k, W:size] = tile
            gram_in[r, k, size:] = diagonal
        swap = start(pltpu.make_async_remote_copy(
            src_ref=gram_in.at[r, 1 - core],
            dst_ref=gram_in.at[r, 2],
            send_sem=swap_send.at[r],
            recv_sem=swap_recv.at[r],
            device_id=row_peers[0],
            device_id_type=MESH,
        ))
        swap.wait_recv()
        total = gram_in[r, core] + gram_in[r, 2]
        for stage in range(stages):
            gram[r, 2 * stage] = total
            pair = []
            for h in range(2):
                bit = (stage + h * (stages // 2)) % stages
                part = pl.ds(0, W) if h == 0 else pl.ds(W, W + 8)
                pair.append(start(pltpu.make_async_remote_copy(
                    src_ref=gram.at[r, 2 * stage, part],
                    dst_ref=gram.at[r, 2 * stage + 1, part],
                    send_sem=sum_send.at[r, stage, h],
                    recv_sem=sum_recv.at[r, stage, h],
                    device_id=row_peers[1 + bit],
                    device_id_type=MESH,
                )))
            for copy in pair:
                copy.wait_recv()
            total = total + gram[r, 2 * stage + 1]
        rot[r, 0] = rotation(unpack(total), eye, stack)
        back = start(pltpu.make_async_remote_copy(
            src_ref=rot.at[r, 0],
            dst_ref=rot.at[r, 1],
            send_sem=rot_send.at[r],
            recv_sem=rot_recv.at[r],
            device_id=row_peers[0],
            device_id_type=MESH,
        ))
        for side in range(2):
            k = core if side == 0 else 1 - core
            if side == 1:
                back.wait_recv()
            for q in range(CHUNKS):
                span = pl.ds(q * chunk, chunk)
                turned = dot3(load_pair(r, k, q), rot[r, side])
                if r == ROUNDS - 1:
                    lanes = pl.ds(pl.multiple_of(k * size, size), size)
                    held[span, lanes] = turned
                    stores.append(pltpu.make_async_copy(
                        held.at[span, lanes], out_ref.at[span, lanes], store_sem.at[side, q]))
                    stores[-1].start()
                else:
                    cur[2 * k, span] = turned[:, :W]
                    cur[2 * k + 1, span] = turned[:, W:]
                    if side == 1:
                        prepare(r + 1, q)
                        for j in range(groups - 1):
                            start(move(r + 1, q, j, g))
    for copy in copies:
        copy.wait_send()
    for copy in stores:
        copy.wait()


def on_device(groups, members, factor, support, plan):
    rows = factor.shape[0]
    slots = factor.shape[1] // W
    chips = members // 2
    stages = chips.bit_length() - 1
    assert slots == 4 and groups == 4 and chips == 1 << stages and stages >= 1 and ROUNDS == 2
    size = 2 * W
    dma = pltpu.SemaphoreType.DMA
    smem = pl.BlockSpec(memory_space=pltpu.SMEM)
    return pl.pallas_call(
        functools.partial(kernel, groups, members),
        out_shape=jax.ShapeDtypeStruct(factor.shape, F32),
        in_specs=[pl.BlockSpec(memory_space=pl.ANY), smem, smem],
        out_specs=pl.BlockSpec(memory_space=pl.ANY),
        scratch_shapes=[
            pltpu.VMEM(factor.shape, F32),
            pltpu.VMEM((slots, rows, W), F32),
            pltpu.VMEM((ROUNDS, groups - 1, rows, W), F32),
            [[pltpu.VMEM((groups, rows // CHUNKS, W), F32)] * CHUNKS] * ROUNDS,
            pltpu.VMEM((2, size, size), F32),
            pltpu.VMEM((ROUNDS, 2 * stages, size + 8, W), F32),
            pltpu.VMEM((ROUNDS, 3, size + 8, W), F32),
            pltpu.VMEM((ROUNDS, 2, size, size), F32),
            pltpu.VMEM((2 * size, size), F32),
            dma((CHUNKS,)),
            dma((2, CHUNKS)),
            dma((ROUNDS, CHUNKS, groups - 1)),
            dma((ROUNDS, CHUNKS, groups)),
            dma((ROUNDS,)),
            dma((ROUNDS,)),
            dma((ROUNDS, stages, 2)),
            dma((ROUNDS, stages, 2)),
            dma((ROUNDS,)),
            dma((ROUNDS,)),
        ],
        compiler_params=pltpu.CompilerParams(
            collective_id=0, has_side_effects=True, vmem_limit_bytes=123 * 512 * 1024
        ),
    )(factor, support.T, plan)


def solution(mesh):
    return jax.shard_map(
        functools.partial(on_device, mesh.shape["col"], mesh.shape["row"]),
        mesh=mesh,
        in_specs=(P("row", "col"), P(None, "row"), P()),
        out_specs=P("row", "col"),
        check_vma=False,
    )
```

time: 129 us -> 125 us (0.969)
  Pallas kernels: 125 us -> 122 us
    pallas_call x1, Pallas kernels: 125 us -> 122 us  [on_device(): pl.pallas_call(functools.partial(kernel, groups, members), out_shape=jax....]
where the time goes in v1:
time: 125 us
  Pallas kernels  122 us (98%)
  local copies, waits for them, and re-layouts  3.08 us (2%)
    pallas_call x1, Pallas kernels, on_device(): pl.pallas_call(functools.partial(kernel, groups, members), out_shape=jax....  122 us
    unnamed x1, local copies, waits for them, and re-layouts  3.08 us

profile of v1, /device:TPU:1, one launch (start us, length us, event | category | flops | bytes accessed | tf_op | source)
XLA Modules:
  0.0 125.3 jit_solution(5795541016905472317)
XLA Ops:
  0.0 122.2 %shard_map.37 = f32[1024,512]{1,0:T(8,128)} custom-call(f32[1024,512]{1,0:T(8,128)} %factor_ref.1, s32[8,16]{1,0:T(8,128)} %bitcast.1, s32[2,16]{1,0:T(2,128)} %plan_ref.1), custom_call_target="tpu_custom_call" | custom-call | tf_op jit(solution)/shard_map/pallas_call | solution.py:296
  122.2 3.1 %copy.5 = f32[1024,512]{1,0:T(8,128)} copy(f32[1024,512]{1,0:T(8,128)} %shard_map.37) | data formatting | bytes 4194304

commit v2 on v1

--- a/solution.py
+++ b/solution.py
@@ -95,8 +95,8 @@
 
 def kernel(
     groups, members, factor_ref, support_ref, plan_ref, out_ref,
-    held, cur, send, recv, acc, gram, gram_in, rot, stack,
-    load_sem, store_sem, move_send, move_recv, swap_send, swap_recv, sum_send, sum_recv, rot_send, rot_recv,
+    held, cur, send, recv, raw_out, raw_in, turn_out, turn, acc, gram, gram_in, rot, stack,
+    load_sem, store_sem, move_send, move_recv, raw_send, raw_recv, turn_send, turn_recv, swap_send, swap_recv, sum_send, sum_recv, rot_send, rot_recv,
 ):
     slots, rows, _ = cur.shape
     size = 2 * W
@@ -109,6 +109,8 @@
     chip = m // 2
     partner = m + 1 - 2 * core
     half = g // 2
+    at_end = jnp.logical_or(g == 0, g == groups - 1)
+    inside = jnp.logical_not(at_end)
     goals = [2 - half, g + 1 - 2 * lax.rem(g, 2), 3 - 3 * half]
 
     def flipped(bit):
@@ -190,8 +192,70 @@
         recv[r][q][g] = cur[keep[r], span]
 
     def arrive(r, q):
-        for o in range(1, groups):
-            move(r, q, 0, lax.rem(g + o, groups)).wait_recv()
+        for s in range(2):
+            move(r, q, 0, 2 - 2 * half + s).wait_recv()
+        if r == 0:
+            move(r, q, 0, goals[1]).wait_recv()
+        else:
+            @pl.when(at_end)
+            def _():
+                move(r, q, 0, goals[1]).wait_recv()
+
+    raws = [pltpu.make_async_remote_copy(
+        src_ref=raw_out.at[q],
+        dst_ref=raw_in.at[q],
+        send_sem=raw_send.at[q],
+        recv_sem=raw_recv.at[q],
+        device_id=goal_peers[1],
+        device_id_type=MESH,
+    ) for q in range(CHUNKS)]
+    near_slot = pick[1][1]
+    share = pl.ds(pl.multiple_of(core * W, W), W)
+    turn_copy = pltpu.make_async_remote_copy(
+        src_ref=turn_out,
+        dst_ref=turn.at[share],
+        send_sem=turn_send.at[0],
+        recv_sem=turn_recv.at[0],
+        device_id=goal_peers[1],
+        device_id_type=MESH,
+    )
+    turn_swap = pltpu.make_async_remote_copy(
+        src_ref=turn.at[share],
+        dst_ref=turn.at[share],
+        send_sem=turn_send.at[1],
+        recv_sem=turn_recv.at[1],
+        device_id=row_peers[0],
+        device_id_type=MESH,
+    )
+
+    def start_raw(q):
+        @pl.when(at_end)
+        def _():
+            raw_out[q] = load_pair(0, near_slot // 2, q)
+            raws[q].start()
+
+    def start_turn():
+        @pl.when(at_end)
+        def _():
+            side = jnp.where(near_slot // 2 == core, 0, 1)
+            wide = rot[0, side, share]
+            turn_out[...] = jnp.where(lax.rem(near_slot, 2) == 0, wide[:, :W], wide[:, W:])
+            turn_copy.start()
+
+    def turn_raws():
+        @pl.when(inside)
+        def _():
+            turn_copy.wait_recv()
+            turn_swap.start()
+            turn_swap.wait_recv()
+            for q in range(CHUNKS):
+                raws[q].wait_recv()
+                recv[1][q][goals[1]] = dot3(raw_in[q], turn[...])
+
+    def start_near(q):
+        @pl.when(inside)
+        def _():
+            move(1, q, 1, g).start()
 
     def load_pair(r, k, q):
         first = jnp.where(k == 0, take[r][0], take[r][2])
@@ -210,8 +274,12 @@
     for q in range(CHUNKS):
         start(move(0, q, groups - 2, g))
     for r in range(ROUNDS):
+        if r == 1:
+            turn_raws()
         for q in range(CHUNKS):
             arrive(r, q)
+            if r == 0:
+                start_raw(q)
             for k in range(2):
                 high, low = split(load_pair(r, k, q))
                 mixed = dot_t(high, low)
@@ -262,6 +330,8 @@
             k = core if side == 0 else 1 - core
             if side == 1:
                 back.wait_recv()
+            if side == 1 and r == 0:
+                start_turn()
             for q in range(CHUNKS):
                 span = pl.ds(q * chunk, chunk)
                 turned = dot3(load_pair(r, k, q), rot[r, side])
@@ -276,8 +346,20 @@
                     cur[2 * k + 1, span] = turned[:, W:]
                     if side == 1:
                         prepare(r + 1, q)
-                        for j in range(groups - 1):
+                        for j in (0, groups - 2):
                             start(move(r + 1, q, j, g))
+                        start_near(q)
+    @pl.when(at_end)
+    def _():
+        for copy in [*raws, turn_copy]:
+            copy.wait_send()
+
+    @pl.when(inside)
+    def _():
+        turn_swap.wait_send()
+        for q in range(CHUNKS):
+            move(1, q, 1, g).wait_send()
+
     for copy in copies:
         copy.wait_send()
     for copy in stores:
@@ -303,6 +385,10 @@
             pltpu.VMEM((slots, rows, W), F32),
             pltpu.VMEM((ROUNDS, groups - 1, rows, W), F32),
             [[pltpu.VMEM((groups, rows // CHUNKS, W), F32)] * CHUNKS] * ROUNDS,
+            pltpu.VMEM((CHUNKS, rows // CHUNKS, size), F32),
+            pltpu.VMEM((CHUNKS, rows // CHUNKS, size), F32),
+            pltpu.VMEM((W, W), F32),
+            pltpu.VMEM((size, W), F32),
             pltpu.VMEM((2, size, size), F32),
             pltpu.VMEM((ROUNDS, 2 * stages, size + 8, W), F32),
             pltpu.VMEM((ROUNDS, 3, size + 8, W), F32),
@@ -312,6 +398,10 @@
             dma((2, CHUNKS)),
             dma((ROUNDS, CHUNKS, groups - 1)),
             dma((ROUNDS, CHUNKS, groups)),
+            dma((CHUNKS,)),
+            dma((CHUNKS,)),
+            dma((2,)),
+            dma((2,)),
             dma((ROUNDS,)),
             dma((ROUNDS,)),
             dma((ROUNDS, stages, 2)),

time: 125 us -> 117 us (0.936)
  Pallas kernels: 122 us -> 114 us
    pallas_call x1, Pallas kernels: 122 us -> 114 us  [on_device(): pl.pallas_call(functools.partial(kernel, groups, members), out_shape=jax....]
where the time goes in v2:
time: 117 us
  Pallas kernels  114 us (97%)
  local copies, waits for them, and re-layouts  3.08 us (3%)
    pallas_call x1, Pallas kernels, on_device(): pl.pallas_call(functools.partial(kernel, groups, members), out_shape=jax....  114 us
    unnamed x1, local copies, waits for them, and re-layouts  3.08 us

profile of v2, /device:TPU:1, one launch (start us, length us, event | category | flops | bytes accessed | tf_op | source)
XLA Modules:
  0.0 117.0 jit_solution(14911090194261071408)
XLA Ops:
  0.0 113.9 %shard_map.37 = f32[1024,512]{1,0:T(8,128)} custom-call(f32[1024,512]{1,0:T(8,128)} %factor_ref.1, s32[8,16]{1,0:T(8,128)} %bitcast.1, s32[2,16]{1,0:T(2,128)} %plan_ref.1), custom_call_target="tpu_custom_call" | custom-call | tf_op jit(solution)/shard_map/pallas_call | solution.py:378
  113.9 3.1 %copy.5 = f32[1024,512]{1,0:T(8,128)} copy(f32[1024,512]{1,0:T(8,128)} %shard_map.37) | data formatting | bytes 4194304

commit v3 on v2

--- a/solution.py
+++ b/solution.py
@@ -96,7 +96,7 @@
 def kernel(
     groups, members, factor_ref, support_ref, plan_ref, out_ref,
     held, cur, send, recv, raw_out, raw_in, turn_out, turn, acc, gram, gram_in, rot, stack,
-    load_sem, store_sem, move_send, move_recv, raw_send, raw_recv, turn_send, turn_recv, swap_send, swap_recv, sum_send, sum_recv, rot_send, rot_recv,
+    load_sem, move_send, move_recv, raw_send, raw_recv, turn_send, turn_recv, swap_send, swap_recv, sum_send, sum_recv, rot_send, rot_recv,
 ):
     slots, rows, _ = cur.shape
     size = 2 * W
@@ -167,7 +167,7 @@
             take[r].append(jnp.minimum(groups - 1, sum(
                 jnp.where(before(r, j) == block, j // slots, 0) for j in range(blocks))))
 
-    copies, stores = [], []
+    copies = []
 
     def start(copy):
         copy.start()
@@ -337,10 +337,7 @@
                 turned = dot3(load_pair(r, k, q), rot[r, side])
                 if r == ROUNDS - 1:
                     lanes = pl.ds(pl.multiple_of(k * size, size), size)
-                    held[span, lanes] = turned
-                    stores.append(pltpu.make_async_copy(
-                        held.at[span, lanes], out_ref.at[span, lanes], store_sem.at[side, q]))
-                    stores[-1].start()
+                    out_ref[span, lanes] = turned
                 else:
                     cur[2 * k, span] = turned[:, :W]
                     cur[2 * k + 1, span] = turned[:, W:]
@@ -362,8 +359,6 @@
 
     for copy in copies:
         copy.wait_send()
-    for copy in stores:
-        copy.wait()
 
 
 def on_device(groups, members, factor, support, plan):
@@ -379,7 +374,7 @@
         functools.partial(kernel, groups, members),
         out_shape=jax.ShapeDtypeStruct(factor.shape, F32),
         in_specs=[pl.BlockSpec(memory_space=pl.ANY), smem, smem],
-        out_specs=pl.BlockSpec(memory_space=pl.ANY),
+        out_specs=pl.BlockSpec(memory_space=pltpu.VMEM),
         scratch_shapes=[
             pltpu.VMEM(factor.shape, F32),
             pltpu.VMEM((slots, rows, W), F32),
@@ -395,7 +390,6 @@
             pltpu.VMEM((ROUNDS, 2, size, size), F32),
             pltpu.VMEM((2 * size, size), F32),
             dma((CHUNKS,)),
-            dma((2, CHUNKS)),
             dma((ROUNDS, CHUNKS, groups - 1)),
             dma((ROUNDS, CHUNKS, groups)),
             dma((CHUNKS,)),
@@ -410,9 +404,9 @@
             dma((ROUNDS,)),
         ],
         compiler_params=pltpu.CompilerParams(
-            collective_id=0, has_side_effects=True, vmem_limit_bytes=123 * 512 * 1024
+            collective_id=0, has_side_effects=True, vmem_limit_bytes=30 * 1024 * 1024
         ),
-    )(factor, support.T, plan)
+    )(*(pltpu.with_memory_space_constraint(x, pltpu.HBM) for x in (factor, support.T, plan)))
 
 
 def solution(mesh):

time: 117 us -> 114 us (0.974)
  local copies, waits for them, and re-layouts: 3.08 us -> 1.32 us
    unnamed x1, local copies, waits for them, and re-layouts: 3.08 us -> 1.32 us
where the time goes in v3:
time: 114 us
  Pallas kernels  113 us (99%)
  local copies, waits for them, and re-layouts  1.32 us (1%)
    pallas_call x1, Pallas kernels, on_device(): pl.pallas_call(functools.partial(kernel, groups, members), out_shape=jax....  113 us

profile of v3, /device:TPU:1, one launch (start us, length us, event | category | flops | bytes accessed | tf_op | source)
XLA Modules:
  0.0 114.3 jit_solution(5385590158269915323)
XLA Ops:
  0.0 113.0 %shard_map.37 = f32[1024,512]{1,0:T(8,128)S(1)} custom-call(f32[1024,512]{1,0:T(8,128)} %factor_ref.1, s32[8,16]{1,0:T(8,128)} %bitcast.1, s32[2,16]{1,0:T(2,128)} %plan_ref.1), custom_call_target="tpu_custom_call" | custom-call | tf_op jit(solution)/shard_map/pallas_call | solution.py:373
  113.0 1.3 %copy.5 = f32[1024,512]{1,0:T(8,128)} copy(f32[1024,512]{1,0:T(8,128)S(1)} %shard_map.37) | data formatting | bytes 4194304

commit v4 on v3

--- a/solution.py
+++ b/solution.py
@@ -11,9 +11,9 @@
 RB = 128
 ROUNDS = 2
 CHUNKS = 4
-SCALED_STEPS = 7
-TRUE_STEPS = 2
+STEPS = 7
 DAMPING = 0.01
+TOP = 2020.0
 F32 = jnp.float32
 BF16 = jnp.bfloat16
 MESH = pl.DeviceIdType.MESH
@@ -47,29 +47,29 @@
     joined = diag_rows + diag_cols
     half = 0.5 * gram * spread / (spread * spread + gram * gram + DAMPING * joined * joined)
     squared = dot3(half, half)
-    total = jnp.sum(jnp.sum(squared * squared, axis=1, keepdims=True), axis=0, keepdims=True)
-    upper = 1.0 + 1.001 * jnp.sqrt(0.5 * total)
     stack[:size] = eye - squared
     stack[size:] = eye - half
-
-    def scaled(_, bounds):
-        low, high = bounds
-        scale = 2.0 / (low + high)
-        delta = (high - low) / (high + low)
-        factor = (2.0 * scale) * eye - (scale * scale) * stack[:size]
-        stack[...] = dot3(stack[...], factor)
-        return 1.0 - delta * delta, jnp.ones_like(high)
-
-    lax.fori_loop(0, SCALED_STEPS, scaled, (jnp.ones_like(upper), upper))
-
-    def true(_, carry):
-        inverse = stack[size:]
-        residual = (eye - inverse) - dot3(half, inverse)
-        stack[size:] = inverse + dot3(inverse, residual)
+    scales, low, high = [], 1.0, TOP
+    for _ in range(STEPS):
+        scales.append(2.0 / (low + high))
+        low, high = 4.0 * low * high / (low + high) ** 2, 1.0
+
+    def factor(scale):
+        return (2.0 * scale) * eye - (scale * scale) * stack[:size]
+
+    def scaled(step, carry):
+        scale = jnp.float32(scales[0])
+        for i in range(1, STEPS - 1):
+            scale = jnp.where(step == i, scales[i], scale)
+        stack[...] = dot3(stack[...], factor(scale))
         return carry
 
-    lax.fori_loop(0, TRUE_STEPS, true, 0)
-    return 2.0 * stack[size:] - eye
+    lax.fori_loop(0, STEPS - 1, scaled, 0)
+    inverse = dot3(stack[size:], factor(scales[-1]))
+    residual = (eye - inverse) - dot3(half, inverse)
+    short = residual.astype(BF16)
+    inverse = inverse + dot3(inverse, residual + dot(short, short))
+    return 2.0 * inverse - eye
 
 
 def pack(gram):

time: 114 us -> 114 us (level)
  no operation moved by 1% of the time
where the time goes in v4:
time: 114 us
  Pallas kernels  112 us (98%)
  local copies, waits for them, and re-layouts  1.32 us (1%)
    pallas_call x1, Pallas kernels, on_device(): pl.pallas_call(functools.partial(kernel, groups, members), out_shape=jax....  112 us

profile of v4, /device:TPU:1, one launch (start us, length us, event | category | flops | bytes accessed | tf_op | source)
XLA Modules:
  0.0 113.6 jit_solution(5901375957969226869)
XLA Ops:
  0.0 112.2 %shard_map.37 = f32[1024,512]{1,0:T(8,128)S(1)} custom-call(f32[1024,512]{1,0:T(8,128)} %factor_ref.1, s32[8,16]{1,0:T(8,128)} %bitcast.1, s32[2,16]{1,0:T(2,128)} %plan_ref.1), custom_call_target="tpu_custom_call" | custom-call | tf_op jit(solution)/shard_map/pallas_call | solution.py:373
  112.3 1.3 %copy.5 = f32[1024,512]{1,0:T(8,128)} copy(f32[1024,512]{1,0:T(8,128)S(1)} %shard_map.37) | data formatting | bytes 4194304

commit v5 on v4

--- a/solution.py
+++ b/solution.py
@@ -13,6 +13,7 @@
 CHUNKS = 4
 STEPS = 7
 DAMPING = 0.01
+RELAY = 128
 TOP = 2020.0
 F32 = jnp.float32
 BF16 = jnp.bfloat16
@@ -81,8 +82,7 @@
     return gram[:W, W:], tile, jnp.broadcast_to(diagonal, (8, W))
 
 
-def unpack(packed):
-    cross, tile, diagonal = packed[:W], packed[W:2 * W], packed[2 * W:2 * W + 1]
+def unpack(cross, tile, diagonal):
     row_ids = lax.broadcasted_iota(jnp.int32, (W, W), 0)
     col_ids = lax.broadcasted_iota(jnp.int32, (W, W), 1)
     lower = jnp.where(row_ids > col_ids, tile, 0.0)
@@ -95,8 +95,9 @@
 
 def kernel(
     groups, members, factor_ref, support_ref, plan_ref, out_ref,
-    held, cur, send, recv, raw_out, raw_in, turn_out, turn, acc, gram, gram_in, rot, stack,
-    load_sem, move_send, move_recv, raw_send, raw_recv, turn_send, turn_recv, swap_send, swap_recv, sum_send, sum_recv, rot_send, rot_recv,
+    held, cur, send, recv, late, relay, raw_out, raw_in, turn_out, turn, acc, gram, gram_in,
+    piece, piece_in, whole, rot, stack,
+    go_sem, relay_send, relay_recv, pass_send, pass_recv, load_sem, move_send, move_recv, raw_send, raw_recv, turn_send, turn_recv, swap_send, swap_recv, sum_send, sum_recv, rot_send, rot_recv, whole_send, whole_recv,
 ):
     slots, rows, _ = cur.shape
     size = 2 * W
@@ -174,32 +175,57 @@
         copies.append(copy)
         return copy
 
-    def move(r, q, j, source):
-        span = pl.ds(q * chunk, chunk)
+    def move(r, q, j, source, last=False):
+        count = chunk - RELAY if last and q == CHUNKS - 1 else chunk
+        landing = late[q] if last else recv[r][q].at[source]
         return pltpu.make_async_remote_copy(
-            src_ref=send.at[r, j, span],
-            dst_ref=recv[r][q].at[source],
+            src_ref=send.at[r, j, pl.ds(q * chunk, count)],
+            dst_ref=landing.at[pl.ds(0, count)],
             send_sem=move_send.at[r, q, j],
             recv_sem=move_recv.at[r, q, source],
             device_id=goal_peers[j],
             device_id_type=MESH,
         )
 
+    across = (0, groups - 2)
+    relays = [pltpu.make_async_remote_copy(
+        src_ref=send.at[1, j, pl.ds(rows - RELAY, RELAY)],
+        dst_ref=relay.at[i],
+        send_sem=relay_send.at[i],
+        recv_sem=relay_recv.at[i],
+        device_id=goal_peers[1],
+        device_id_type=MESH,
+    ) for i, j in enumerate(across)]
+    passes = [pltpu.make_async_remote_copy(
+        src_ref=relay.at[i],
+        dst_ref=late[CHUNKS - 1].at[pl.ds(chunk - RELAY, RELAY)],
+        send_sem=pass_send.at[i],
+        recv_sem=pass_recv.at[0],
+        device_id=goal_peers[j],
+        device_id_type=MESH,
+    ) for i, j in enumerate(across)]
+
     def prepare(r, q):
         span = pl.ds(q * chunk, chunk)
         for j in range(groups - 1):
             send[r, j, span] = cur[pick[r][j], span]
         recv[r][q][g] = cur[keep[r], span]
 
-    def arrive(r, q):
-        for s in range(2):
-            move(r, q, 0, 2 - 2 * half + s).wait_recv()
-        if r == 0:
-            move(r, q, 0, goals[1]).wait_recv()
-        else:
-            @pl.when(at_end)
-            def _():
-                move(r, q, 0, goals[1]).wait_recv()
+    def arrive_first(q):
+        for source in goals:
+            move(0, q, 0, source).wait_recv()
+
+    def arrive_early(q):
+        move(1, q, 0, goals[0]).wait_recv()
+
+        @pl.when(at_end)
+        def _():
+            move(1, q, 0, goals[1]).wait_recv()
+
+    def arrive_late(q):
+        move(1, q, 0, goals[2], True).wait_recv()
+        if q == CHUNKS - 1:
+            passes[0].wait_recv()
 
     raws = [pltpu.make_async_remote_copy(
         src_ref=raw_out.at[q],
@@ -231,14 +257,14 @@
     def start_raw(q):
         @pl.when(at_end)
         def _():
-            raw_out[q] = load_pair(0, near_slot // 2, q)
+            raw_out[q] = load_pair(near_slot // 2, q)
             raws[q].start()
 
     def start_turn():
         @pl.when(at_end)
         def _():
             side = jnp.where(near_slot // 2 == core, 0, 1)
-            wide = rot[0, side, share]
+            wide = rot[side, share]
             turn_out[...] = jnp.where(lax.rem(near_slot, 2) == 0, wide[:, :W], wide[:, W:])
             turn_copy.start()
 
@@ -252,15 +278,107 @@
                 raws[q].wait_recv()
                 recv[1][q][goals[1]] = dot3(raw_in[q], turn[...])
 
-    def start_near(q):
+    def start_second(q):
         @pl.when(inside)
         def _():
-            move(1, q, 1, g).start()
-
-    def load_pair(r, k, q):
-        first = jnp.where(k == 0, take[r][0], take[r][2])
-        last = jnp.where(k == 0, take[r][1], take[r][3])
-        return jnp.concatenate([recv[r][q][first], recv[r][q][last]], axis=1)
+            for j in range(groups - 1):
+                move(1, q, j, g).start()
+
+        if q == CHUNKS - 1:
+            @pl.when(at_end)
+            def _():
+                for copy in relays:
+                    copy.start()
+
+    def start_far():
+        @pl.when(inside)
+        def _():
+            for q in range(CHUNKS):
+                for j in across:
+                    move(1, q, j, g).wait_send()
+            pl.semaphore_signal(go_sem.at[1], inc=1, device_id=goal_peers[1], device_id_type=MESH)
+            for i in range(2):
+                relays[i].wait_recv()
+                passes[i].start()
+
+        @pl.when(at_end)
+        def _():
+            pl.semaphore_wait(go_sem.at[1], 1)
+            for q in range(CHUNKS):
+                for j in across:
+                    move(1, q, j, g, True).start()
+
+    def load_pair(k, q):
+        first = jnp.where(k == 0, take[0][0], take[0][2])
+        last = jnp.where(k == 0, take[0][1], take[0][3])
+        return jnp.concatenate([recv[0][q][first], recv[0][q][last]], axis=1)
+
+    far = goals[2]
+    late_last = jnp.logical_or(take[1][2] == far, take[1][3] == far)
+    late_pair = [jnp.where(late_last, take[1][2 + i], take[1][i]) for i in range(2)]
+    early_pair = [jnp.where(late_last, take[1][i], take[1][2 + i]) for i in range(2)]
+    far_left = late_pair[0] == far
+    late_other = jnp.where(far_left, late_pair[1], late_pair[0])
+
+    def load_early(q):
+        return jnp.concatenate([recv[1][q][block] for block in early_pair], axis=1)
+
+    def load_late(q):
+        newest, other = late[q][...], recv[1][q][late_other]
+        left, right = jnp.where(far_left, newest, other), jnp.where(far_left, other, newest)
+        return jnp.concatenate([left, right], axis=1)
+
+    def add_gram(k, q, pair):
+        high, low = split(pair)
+        mixed = dot_t(high, low)
+        part = dot_t(high, high) + (mixed + mixed.T)
+        acc[k] = part if q == 0 else acc[k] + part
+
+    def sum_chips(phase, total, slots_ref, cut):
+        for stage in range(stages):
+            slots_ref[2 * stage] = total
+            both = []
+            for h in range(2):
+                bit = (stage + h * (stages // 2)) % stages
+                part = pl.ds(0, cut) if h == 0 else pl.ds(cut, total.shape[0] - cut)
+                both.append(start(pltpu.make_async_remote_copy(
+                    src_ref=slots_ref.at[2 * stage, part],
+                    dst_ref=slots_ref.at[2 * stage + 1, part],
+                    send_sem=sum_send.at[phase, stage, h],
+                    recv_sem=sum_recv.at[phase, stage, h],
+                    device_id=row_peers[1 + bit],
+                    device_id_type=MESH,
+                )))
+            for copy in both:
+                copy.wait_recv()
+            total = total + slots_ref[2 * stage + 1]
+        return total
+
+    def rotation_of(e):
+        cross, tile, diagonal = pack(acc[e])
+        piece_in[e, 0, :W] = cross
+        piece_in[e, 0, W:] = diagonal
+        piece_in[e, 1, :W] = tile
+        piece_in[e, 1, W:] = diagonal
+        start(pltpu.make_async_remote_copy(
+            src_ref=piece_in.at[e, 1 - core],
+            dst_ref=piece_in.at[e, 2],
+            send_sem=swap_send.at[1 + e],
+            recv_sem=swap_recv.at[1 + e],
+            device_id=row_peers[0],
+            device_id_type=MESH,
+        )).wait_recv()
+        total = sum_chips(1 + e, piece_in[e, core] + piece_in[e, 2], piece.at[e], W // 2)
+        whole[e, core] = total
+        start(pltpu.make_async_remote_copy(
+            src_ref=whole.at[e, core],
+            dst_ref=whole.at[e, core],
+            send_sem=whole_send.at[e],
+            recv_sem=whole_recv.at[e],
+            device_id=row_peers[0],
+            device_id_type=MESH,
+        )).wait_recv()
+        return rotation(unpack(whole[e, 0, :W], whole[e, 1, :W], whole[e, 0, W:W + 1]), eye, stack)
 
     mask(0)
     prepare(0, 0)
@@ -271,81 +389,80 @@
             prepare(0, q)
         for j in range(groups - 2):
             start(move(0, q, j, g))
-    for q in range(CHUNKS):
-        start(move(0, q, groups - 2, g))
-    for r in range(ROUNDS):
-        if r == 1:
-            turn_raws()
+    @pl.when(at_end)
+    def _():
+        pl.semaphore_wait(go_sem.at[0], 1)
         for q in range(CHUNKS):
-            arrive(r, q)
-            if r == 0:
-                start_raw(q)
-            for k in range(2):
-                high, low = split(load_pair(r, k, q))
-                mixed = dot_t(high, low)
-                part = dot_t(high, high) + (mixed + mixed.T)
-                acc[k] = part if q == 0 else acc[k] + part
+            move(0, q, groups - 2, g).start()
+
+    for q in range(CHUNKS):
+        arrive_first(q)
+        if q == CHUNKS - 2:
+            @pl.when(inside)
+            def _():
+                for c in range(CHUNKS):
+                    move(0, c, groups - 2, g).start()
+        if q == CHUNKS - 1:
+            @pl.when(inside)
+            def _():
+                pl.semaphore_signal(go_sem.at[0], inc=1, device_id=goal_peers[1], device_id_type=MESH)
+        start_raw(q)
         for k in range(2):
-            cross, tile, diagonal = pack(acc[k])
-            gram_in[r, k, :W] = cross
-            gram_in[r, k, W:size] = tile
-            gram_in[r, k, size:] = diagonal
-        swap = start(pltpu.make_async_remote_copy(
-            src_ref=gram_in.at[r, 1 - core],
-            dst_ref=gram_in.at[r, 2],
-            send_sem=swap_send.at[r],
-            recv_sem=swap_recv.at[r],
-            device_id=row_peers[0],
-            device_id_type=MESH,
-        ))
-        swap.wait_recv()
-        total = gram_in[r, core] + gram_in[r, 2]
-        for stage in range(stages):
-            gram[r, 2 * stage] = total
-            pair = []
-            for h in range(2):
-                bit = (stage + h * (stages // 2)) % stages
-                part = pl.ds(0, W) if h == 0 else pl.ds(W, W + 8)
-                pair.append(start(pltpu.make_async_remote_copy(
-                    src_ref=gram.at[r, 2 * stage, part],
-                    dst_ref=gram.at[r, 2 * stage + 1, part],
-                    send_sem=sum_send.at[r, stage, h],
-                    recv_sem=sum_recv.at[r, stage, h],
-                    device_id=row_peers[1 + bit],
-                    device_id_type=MESH,
-                )))
-            for copy in pair:
-                copy.wait_recv()
-            total = total + gram[r, 2 * stage + 1]
-        rot[r, 0] = rotation(unpack(total), eye, stack)
-        back = start(pltpu.make_async_remote_copy(
-            src_ref=rot.at[r, 0],
-            dst_ref=rot.at[r, 1],
-            send_sem=rot_send.at[r],
-            recv_sem=rot_recv.at[r],
-            device_id=row_peers[0],
-            device_id_type=MESH,
-        ))
-        for side in range(2):
-            k = core if side == 0 else 1 - core
+            add_gram(k, q, load_pair(k, q))
+    for k in range(2):
+        cross, tile, diagonal = pack(acc[k])
+        gram_in[k, :W] = cross
+        gram_in[k, W:size] = tile
+        gram_in[k, size:] = diagonal
+    start(pltpu.make_async_remote_copy(
+        src_ref=gram_in.at[1 - core],
+        dst_ref=gram_in.at[2],
+        send_sem=swap_send.at[0],
+        recv_sem=swap_recv.at[0],
+        device_id=row_peers[0],
+        device_id_type=MESH,
+    )).wait_recv()
+    total = sum_chips(0, gram_in[core] + gram_in[2], gram, W)
+    rot[0] = rotation(unpack(total[:W], total[W:size], total[size:size + 1]), eye, stack)
+    back = start(pltpu.make_async_remote_copy(
+        src_ref=rot.at[0],
+        dst_ref=rot.at[1],
+        send_sem=rot_send.at[0],
+        recv_sem=rot_recv.at[0],
+        device_id=row_peers[0],
+        device_id_type=MESH,
+    ))
+    for side in range(2):
+        k = core if side == 0 else 1 - core
+        if side == 1:
+            back.wait_recv()
+            start_turn()
+        for q in (CHUNKS - 1, *range(CHUNKS - 1)):
+            span = pl.ds(q * chunk, chunk)
+            turned = dot3(load_pair(k, q), rot[side])
+            cur[2 * k, span] = turned[:, :W]
+            cur[2 * k + 1, span] = turned[:, W:]
             if side == 1:
-                back.wait_recv()
-            if side == 1 and r == 0:
-                start_turn()
-            for q in range(CHUNKS):
-                span = pl.ds(q * chunk, chunk)
-                turned = dot3(load_pair(r, k, q), rot[r, side])
-                if r == ROUNDS - 1:
-                    lanes = pl.ds(pl.multiple_of(k * size, size), size)
-                    out_ref[span, lanes] = turned
-                else:
-                    cur[2 * k, span] = turned[:, :W]
-                    cur[2 * k + 1, span] = turned[:, W:]
-                    if side == 1:
-                        prepare(r + 1, q)
-                        for j in (0, groups - 2):
-                            start(move(r + 1, q, j, g))
-                        start_near(q)
+                prepare(1, q)
+                start_second(q)
+
+    start_far()
+    turn_raws()
+    for q in range(CHUNKS):
+        arrive_early(q)
+        add_gram(0, q, load_early(q))
+    early = rotation_of(0)
+    for q in range(CHUNKS):
+        held[pl.ds(q * chunk, chunk), :size] = dot3(load_early(q), early)
+    for q in range(CHUNKS):
+        arrive_late(q)
+        add_gram(1, q, load_late(q))
+    last = rotation_of(1)
+    for q in range(CHUNKS):
+        span = pl.ds(q * chunk, chunk)
+        turned, ready = dot3(load_late(q), last), held[span, :size]
+        out_ref[span, :size] = jnp.where(late_last, ready, turned)
+        out_ref[span, size:] = jnp.where(late_last, turned, ready)
     @pl.when(at_end)
     def _():
         for copy in [*raws, turn_copy]:
@@ -354,8 +471,21 @@
     @pl.when(inside)
     def _():
         turn_swap.wait_send()
+        for copy in passes:
+            copy.wait_send()
         for q in range(CHUNKS):
             move(1, q, 1, g).wait_send()
+
+    for q in range(CHUNKS):
+        move(0, q, groups - 2, g).wait_send()
+
+    @pl.when(at_end)
+    def _():
+        for q in range(CHUNKS):
+            for j in across:
+                move(1, q, j, g, True).wait_send()
+        for copy in relays:
+            copy.wait_send()
 
     for copy in copies:
         copy.wait_send()
@@ -380,15 +510,25 @@
             pltpu.VMEM((slots, rows, W), F32),
             pltpu.VMEM((ROUNDS, groups - 1, rows, W), F32),
             [[pltpu.VMEM((groups, rows // CHUNKS, W), F32)] * CHUNKS] * ROUNDS,
+            [pltpu.VMEM((rows // CHUNKS, W), F32)] * CHUNKS,
+            pltpu.VMEM((2, RELAY, W), F32),
             pltpu.VMEM((CHUNKS, rows // CHUNKS, size), F32),
             pltpu.VMEM((CHUNKS, rows // CHUNKS, size), F32),
             pltpu.VMEM((W, W), F32),
             pltpu.VMEM((size, W), F32),
             pltpu.VMEM((2, size, size), F32),
-            pltpu.VMEM((ROUNDS, 2 * stages, size + 8, W), F32),
-            pltpu.VMEM((ROUNDS, 3, size + 8, W), F32),
-            pltpu.VMEM((ROUNDS, 2, size, size), F32),
+            pltpu.VMEM((2 * stages, size + 8, W), F32),
+            pltpu.VMEM((3, size + 8, W), F32),
+            pltpu.VMEM((2, 2 * stages, W + 8, W), F32),
+            pltpu.VMEM((2, 3, W + 8, W), F32),
+            pltpu.VMEM((2, 2, W + 8, W), F32),
+            pltpu.VMEM((2, size, size), F32),
             pltpu.VMEM((2 * size, size), F32),
+            pltpu.SemaphoreType.REGULAR((2,)),
+            dma((2,)),
+            dma((2,)),
+            dma((2,)),
+            dma((1,)),
             dma((CHUNKS,)),
             dma((ROUNDS, CHUNKS, groups - 1)),
             dma((ROUNDS, CHUNKS, groups)),
@@ -396,12 +536,14 @@
             dma((CHUNKS,)),
             dma((2,)),
             dma((2,)),
-            dma((ROUNDS,)),
-            dma((ROUNDS,)),
-            dma((ROUNDS, stages, 2)),
-            dma((ROUNDS, stages, 2)),
-            dma((ROUNDS,)),
-            dma((ROUNDS,)),
+            dma((3,)),
+            dma((3,)),
+            dma((3, stages, 2)),
+            dma((3, stages, 2)),
+            dma((1,)),
+            dma((1,)),
+            dma((2,)),
+            dma((2,)),
         ],
         compiler_params=pltpu.CompilerParams(
             collective_id=0, has_side_effects=True, vmem_limit_bytes=30 * 1024 * 1024

time: 114 us -> 112 us (0.982)
    pallas_call x1, Pallas kernels: 112 us -> 111 us  [on_device(): pl.pallas_call(functools.partial(kernel, groups, members), out_shape=jax....]
where the time goes in v5:
time: 112 us
  Pallas kernels  111 us (99%)
  local copies, waits for them, and re-layouts  1.32 us (1%)
    pallas_call x1, Pallas kernels, on_device(): pl.pallas_call(functools.partial(kernel, groups, members), out_shape=jax....  111 us

profile of v5, /device:TPU:1, one launch (start us, length us, event | category | flops | bytes accessed | tf_op | source)
XLA Modules:
  0.0 112.2 jit_solution(4407654293628587627)
XLA Ops:
  0.0 110.8 %shard_map.37 = f32[1024,512]{1,0:T(8,128)S(1)} custom-call(f32[1024,512]{1,0:T(8,128)} %factor_ref.1, s32[8,16]{1,0:T(8,128)} %bitcast.1, s32[2,16]{1,0:T(2,128)} %plan_ref.1), custom_call_target="tpu_custom_call" | custom-call | tf_op jit(solution)/shard_map/pallas_call | solution.py:503
  110.8 1.3 %copy.5 = f32[1024,512]{1,0:T(8,128)} copy(f32[1024,512]{1,0:T(8,128)S(1)} %shard_map.37) | data formatting | bytes 4194304

commit v6 on v5

--- a/solution.py
+++ b/solution.py
@@ -97,7 +97,7 @@
     groups, members, factor_ref, support_ref, plan_ref, out_ref,
     held, cur, send, recv, late, relay, raw_out, raw_in, turn_out, turn, acc, gram, gram_in,
     piece, piece_in, whole, rot, stack,
-    go_sem, relay_send, relay_recv, pass_send, pass_recv, load_sem, move_send, move_recv, raw_send, raw_recv, turn_send, turn_recv, swap_send, swap_recv, sum_send, sum_recv, rot_send, rot_recv, whole_send, whole_recv,
+    go_sem, relay_send, relay_recv, pass_send, pass_recv, load_sem, move_send, move_recv, raw_send, raw_recv, turn_send, turn_recv, swap_send, swap_recv, sum_send, sum_recv, quad_send, quad_recv, rot_send, rot_recv, whole_send, whole_recv,
 ):
     slots, rows, _ = cur.shape
     size = 2 * W
@@ -128,8 +128,14 @@
     goal_peers = [{"col": goal, "row": m} for goal in goals]
     row_peers = [{"col": g, "row": partner}]
     row_peers += [{"col": g, "row": flipped(b)} for b in range(stages)]
+    quads = stages // 2
+    quad_peers = []
+    for b in range(quads):
+        one, two = flipped(b), flipped(b + quads)
+        quad_peers.append([{"col": g, "row": other} for other in (one, two, one + two - m)])
+    diagonals = [quad[2] for quad in quad_peers]
     barrier = pltpu.get_barrier_semaphore()
-    for peer in goal_peers + row_peers:
+    for peer in goal_peers + row_peers + diagonals:
         pl.semaphore_signal(barrier, inc=1, device_id=peer, device_id_type=MESH)
 
     row_ids = lax.broadcasted_iota(jnp.int32, (size, size), 0)
@@ -334,7 +340,7 @@
         part = dot_t(high, high) + (mixed + mixed.T)
         acc[k] = part if q == 0 else acc[k] + part
 
-    def sum_chips(phase, total, slots_ref, cut):
+    def sum_chips(total, slots_ref, cut):
         for stage in range(stages):
             slots_ref[2 * stage] = total
             both = []
@@ -344,14 +350,31 @@
                 both.append(start(pltpu.make_async_remote_copy(
                     src_ref=slots_ref.at[2 * stage, part],
                     dst_ref=slots_ref.at[2 * stage + 1, part],
-                    send_sem=sum_send.at[phase, stage, h],
-                    recv_sem=sum_recv.at[phase, stage, h],
+                    send_sem=sum_send.at[stage, h],
+                    recv_sem=sum_recv.at[stage, h],
                     device_id=row_peers[1 + bit],
                     device_id_type=MESH,
                 )))
             for copy in both:
                 copy.wait_recv()
             total = total + slots_ref[2 * stage + 1]
+        return total
+
+    def sum_quads(e, total):
+        for step in range(quads):
+            piece[e, 4 * step] = total
+            three = [start(pltpu.make_async_remote_copy(
+                src_ref=piece.at[e, 4 * step],
+                dst_ref=piece.at[e, 4 * step + 1 + i],
+                send_sem=quad_send.at[e, step, i],
+                recv_sem=quad_recv.at[e, step, i],
+                device_id=quad_peers[step][i],
+                device_id_type=MESH,
+            )) for i in (2, 0, 1)]
+            for copy in three:
+                copy.wait_recv()
+            pair, other = (piece[e, 4 * step + 2 * i] + piece[e, 4 * step + 2 * i + 1] for i in range(2))
+            total = pair + other
         return total
 
     def rotation_of(e):
@@ -368,7 +391,7 @@
             device_id=row_peers[0],
             device_id_type=MESH,
         )).wait_recv()
-        total = sum_chips(1 + e, piece_in[e, core] + piece_in[e, 2], piece.at[e], W // 2)
+        total = sum_quads(e, piece_in[e, core] + piece_in[e, 2])
         whole[e, core] = total
         start(pltpu.make_async_remote_copy(
             src_ref=whole.at[e, core],
@@ -382,7 +405,7 @@
 
     mask(0)
     prepare(0, 0)
-    pl.semaphore_wait(barrier, groups - 1 + len(row_peers))
+    pl.semaphore_wait(barrier, groups - 1 + len(row_peers) + quads)
     for q in range(CHUNKS):
         if q:
             mask(q)
@@ -422,7 +445,7 @@
         device_id=row_peers[0],
         device_id_type=MESH,
     )).wait_recv()
-    total = sum_chips(0, gram_in[core] + gram_in[2], gram, W)
+    total = sum_chips(gram_in[core] + gram_in[2], gram, W)
     rot[0] = rotation(unpack(total[:W], total[W:size], total[size:size + 1]), eye, stack)
     back = start(pltpu.make_async_remote_copy(
         src_ref=rot.at[0],
@@ -496,7 +519,7 @@
     slots = factor.shape[1] // W
     chips = members // 2
     stages = chips.bit_length() - 1
-    assert slots == 4 and groups == 4 and chips == 1 << stages and stages >= 1 and ROUNDS == 2
+    assert slots == 4 and groups == 4 and chips == 1 << stages and stages % 2 == 0 and ROUNDS == 2
     size = 2 * W
     dma = pltpu.SemaphoreType.DMA
     smem = pl.BlockSpec(memory_space=pltpu.SMEM)
@@ -538,8 +561,10 @@
             dma((2,)),
             dma((3,)),
             dma((3,)),
-            dma((3, stages, 2)),
-            dma((3, stages, 2)),
+            dma((stages, 2)),
+            dma((stages, 2)),
+            dma((2, stages // 2, 3)),
+            dma((2, stages // 2, 3)),
             dma((1,)),
             dma((1,)),
             dma((2,)),

time: 112 us -> 111 us (level)
  Pallas kernels: 111 us -> 109 us
    pallas_call x1, Pallas kernels: 111 us -> 109 us  [on_device(): pl.pallas_call(functools.partial(kernel, groups, members), out_shape=jax....]
where the time goes in v6:
time: 111 us
  Pallas kernels  109 us (98%)
  local copies, waits for them, and re-layouts  1.32 us (1%)
    pallas_call x1, Pallas kernels, on_device(): pl.pallas_call(functools.partial(kernel, groups, members), out_shape=jax....  109 us

profile of v6, /device:TPU:1, one launch (start us, length us, event | category | flops | bytes accessed | tf_op | source)
XLA Modules:
  0.0 110.6 jit_solution(2409173029312255675)
XLA Ops:
  0.0 109.3 %shard_map.37 = f32[1024,512]{1,0:T(8,128)S(1)} custom-call(f32[1024,512]{1,0:T(8,128)} %factor_ref.1, s32[8,16]{1,0:T(8,128)} %bitcast.1, s32[2,16]{1,0:T(2,128)} %plan_ref.1), custom_call_target="tpu_custom_call" | custom-call | tf_op jit(solution)/shard_map/pallas_call | solution.py:526
  109.3 1.3 %copy.5 = f32[1024,512]{1,0:T(8,128)} copy(f32[1024,512]{1,0:T(8,128)S(1)} %shard_map.37) | data formatting | bytes 4194304

commit v7 on v6

--- a/solution.py
+++ b/solution.py
@@ -13,7 +13,7 @@
 CHUNKS = 4
 STEPS = 7
 DAMPING = 0.01
-RELAY = 128
+RELAY = 160
 TOP = 2020.0
 F32 = jnp.float32
 BF16 = jnp.bfloat16
@@ -287,7 +287,7 @@
     def start_second(q):
         @pl.when(inside)
         def _():
-            for j in range(groups - 1):
+            for j in (*across, 1):
                 move(1, q, j, g).start()
 
         if q == CHUNKS - 1:
@@ -459,7 +459,6 @@
         k = core if side == 0 else 1 - core
         if side == 1:
             back.wait_recv()
-            start_turn()
         for q in (CHUNKS - 1, *range(CHUNKS - 1)):
             span = pl.ds(q * chunk, chunk)
             turned = dot3(load_pair(k, q), rot[side])
@@ -468,6 +467,8 @@
             if side == 1:
                 prepare(1, q)
                 start_second(q)
+                if q == CHUNKS - 1:
+                    start_turn()
 
     start_far()
     turn_raws()

time: 111 us -> 111 us (level)
  no operation moved by 1% of the time
where the time goes in v7:
time: 111 us
  Pallas kernels  109 us (98%)
  local copies, waits for them, and re-layouts  1.32 us (1%)
    pallas_call x1, Pallas kernels, on_device(): pl.pallas_call(functools.partial(kernel, groups, members), out_shape=jax....  109 us

profile of v7, /device:TPU:1, one launch (start us, length us, event | category | flops | bytes accessed | tf_op | source)
XLA Modules:
  0.0 110.6 jit_solution(2602777454835846607)
XLA Ops:
  0.0 109.3 %shard_map.37 = f32[1024,512]{1,0:T(8,128)S(1)} custom-call(f32[1024,512]{1,0:T(8,128)} %factor_ref.1, s32[8,16]{1,0:T(8,128)} %bitcast.1, s32[2,16]{1,0:T(2,128)} %plan_ref.1), custom_call_target="tpu_custom_call" | custom-call | tf_op jit(solution)/shard_map/pallas_call | solution.py:527
  109.3 1.3 %copy.5 = f32[1024,512]{1,0:T(8,128)} copy(f32[1024,512]{1,0:T(8,128)S(1)} %shard_map.37) | data formatting | bytes 4194304

commit v8 on v7

--- a/solution.py
+++ b/solution.py
@@ -95,7 +95,7 @@
 
 def kernel(
     groups, members, factor_ref, support_ref, plan_ref, out_ref,
-    held, cur, send, recv, late, relay, raw_out, raw_in, turn_out, turn, acc, gram, gram_in,
+    held, cur, send, recv, late, relay, halves, raw_out, raw_in, turn_out, turn, acc, gram, gram_in,
     piece, piece_in, whole, rot, stack,
     go_sem, relay_send, relay_recv, pass_send, pass_recv, load_sem, move_send, move_recv, raw_send, raw_recv, turn_send, turn_recv, swap_send, swap_recv, sum_send, sum_recv, quad_send, quad_recv, rot_send, rot_recv, whole_send, whole_recv,
 ):
@@ -480,11 +480,14 @@
         held[pl.ds(q * chunk, chunk), :size] = dot3(load_early(q), early)
     for q in range(CHUNKS):
         arrive_late(q)
-        add_gram(1, q, load_late(q))
-    last = rotation_of(1)
+        pair = load_late(q)
+        add_gram(1, q, pair)
+        halves[0, q], halves[1, q] = split(pair)
+    last_high, last_low = split(rotation_of(1))
     for q in range(CHUNKS):
         span = pl.ds(q * chunk, chunk)
-        turned, ready = dot3(load_late(q), last), held[span, :size]
+        high, low, ready = halves[0, q], halves[1, q], held[span, :size]
+        turned = dot(high, last_high) + (dot(high, last_low) + dot(low, last_high))
         out_ref[span, :size] = jnp.where(late_last, ready, turned)
         out_ref[span, size:] = jnp.where(late_last, turned, ready)
     @pl.when(at_end)
@@ -536,6 +539,7 @@
             [[pltpu.VMEM((groups, rows // CHUNKS, W), F32)] * CHUNKS] * ROUNDS,
             [pltpu.VMEM((rows // CHUNKS, W), F32)] * CHUNKS,
             pltpu.VMEM((2, RELAY, W), F32),
+            pltpu.VMEM((2, CHUNKS, rows // CHUNKS, size), BF16),
             pltpu.VMEM((CHUNKS, rows // CHUNKS, size), F32),
             pltpu.VMEM((CHUNKS, rows // CHUNKS, size), F32),
             pltpu.VMEM((W, W), F32),

time: 111 us -> 111 us (level)
  no operation moved by 1% of the time
where the time goes in v8:
time: 111 us
  Pallas kernels  109 us (98%)
  local copies, waits for them, and re-layouts  1.32 us (1%)
    pallas_call x1, Pallas kernels, on_device(): pl.pallas_call(functools.partial(kernel, groups, members), out_shape=jax....  109 us

profile of v8, /device:TPU:1, one launch (start us, length us, event | category | flops | bytes accessed | tf_op | source)
XLA Modules:
  0.0 110.6 jit_solution(16858695908647949478)
XLA Ops:
  0.0 109.3 %shard_map.37 = f32[1024,512]{1,0:T(8,128)S(1)} custom-call(f32[1024,512]{1,0:T(8,128)} %factor_ref.1, s32[8,16]{1,0:T(8,128)} %bitcast.1, s32[2,16]{1,0:T(2,128)} %plan_ref.1), custom_call_target="tpu_custom_call" | custom-call | tf_op jit(solution)/shard_map/pallas_call | solution.py:530
  109.3 1.3 %copy.5 = f32[1024,512]{1,0:T(8,128)} copy(f32[1024,512]{1,0:T(8,128)S(1)} %shard_map.37) | data formatting | bytes 4194304

commit v9 on v8

--- a/solution.py
+++ b/solution.py
@@ -10,7 +10,7 @@
 W = 128
 RB = 128
 ROUNDS = 2
-CHUNKS = 4
+CHUNKS = 2
 STEPS = 7
 DAMPING = 0.01
 RELAY = 160

time: 111 us -> 111 us (level)
  no operation moved by 1% of the time
where the time goes in v9:
time: 111 us
  Pallas kernels  109 us (98%)
  local copies, waits for them, and re-layouts  1.32 us (1%)
    pallas_call x1, Pallas kernels, on_device(): pl.pallas_call(functools.partial(kernel, groups, members), out_shape=jax....  109 us

profile of v9, /device:TPU:1, one launch (start us, length us, event | category | flops | bytes accessed | tf_op | source)
XLA Modules:
  0.0 110.6 jit_solution(14801274363733668013)
XLA Ops:
  0.0 109.3 %shard_map.37 = f32[1024,512]{1,0:T(8,128)S(1)} custom-call(f32[1024,512]{1,0:T(8,128)} %factor_ref.1, s32[8,16]{1,0:T(8,128)} %bitcast.1, s32[2,16]{1,0:T(2,128)} %plan_ref.1), custom_call_target="tpu_custom_call" | custom-call | tf_op jit(solution)/shard_map/pallas_call | solution.py:530
  109.3 1.3 %copy.5 = f32[1024,512]{1,0:T(8,128)} copy(f32[1024,512]{1,0:T(8,128)S(1)} %shard_map.37) | data formatting | bytes 4194304
